TPU v7x, 512 devices: a whole 4x8x8 slice. The times are simulated.
512 devices in a mesh: dp: 32 (over x, z), fsdp: 16 (over y, core).
Axes of the slice: x: 4, y: 8, z: 8, core: 2. Of those that a mesh axis runs over, the one named last changes fastest.
Arguments:
- hidden: bfloat16 [32768, 16, 1024], P(('dp', 'fsdp')), may hold values from -108 to 108
- head: bfloat16 [16, 1024, 1024], P('fsdp', 'dp'), may hold values from -14 to 14
- gain: bfloat16 [16, 1024], P('fsdp', 'dp'), may hold values from 0.5 to 1.5
- targets: int32 [32768, 16], P('dp', 'fsdp'), may hold values from 0 to 1023
- lengths: int32 [32], replicated, may hold values from 256 to 1024, as said below
Outputs:
- loss: float32 [], replicated
- grad_hidden: bfloat16 [32768, 16, 1024], P(('dp', 'fsdp'))
- grad_head: float32 [16, 1024, 1024], P('fsdp', 'dp')
Inputs may be any that keep to these rules, and one draw needn't show every extreme that they name: `lengths`: each dialogue has at least 256 valid frames, and some dialogue has all 1024.
All inputs are finite; a program needn't handle non-finite values.
Results may differ from a plain program's by a relative error of at most 0.015.
Values may be sent and summed in bfloat16 or wider, within the bound.
A program may use at most 64 MiB of HBM per device.

v0:
```python
import jax
import jax.numpy as jnp
from jax import lax
from jax.sharding import PartitionSpec as P

EPS = 1e-05


def per_device(hidden, head, gain, targets, lengths):
    rows = lax.all_to_all(hidden, "fsdp", split_axis=1, concat_axis=0, tiled=True)
    rows = rows[:, 0, :]
    labels = targets[:, 0]
    frames = rows.shape[0]
    classes = head.shape[2]
    dialogue = lax.axis_index("dp")
    dialog_ids = jnp.arange(lengths.shape[0], dtype=jnp.int32)
    length = jnp.sum(jnp.where(dialog_ids == dialogue, lengths, 0))
    valid = (jnp.arange(frames, dtype=jnp.int32) < length).astype(jnp.float32)
    widened = rows.astype(jnp.float32)
    inverse = lax.rsqrt(jnp.mean(widened * widened, axis=1, keepdims=True) + EPS)
    scaled = widened * inverse
    weights = lax.all_gather(head[0], "dp", axis=0, tiled=True)
    gains = lax.all_gather(gain[0], "dp", axis=0, tiled=True)
    gains_wide = gains.astype(jnp.float32)
    columns = scaled
    piece_normed = (columns * gains_wide[None, :]).astype(jnp.bfloat16)
    logit_sum = jnp.dot(piece_normed, weights, preferred_element_type=jnp.float32)
    top = jnp.max(logit_sum, axis=1, keepdims=True)
    shifted = logit_sum - top
    total = jnp.sum(jnp.exp(shifted), axis=1, keepdims=True)
    log_total = top + jnp.log(total)
    onehot = (labels[:, None] == jnp.arange(classes, dtype=jnp.int32)[None, :]).astype(jnp.float32)
    picked = jnp.sum(logit_sum * onehot, axis=1)
    local = jnp.sum(valid * (log_total[:, 0] - picked))
    summed = lax.psum(local, ("dp", "fsdp"))
    loss = summed / (jnp.sum(lengths).astype(jnp.float32) * lax.axis_size("fsdp"))
    probs = jnp.exp(shifted) / total
    slopes = (valid[:, None] * (probs - onehot)).astype(jnp.bfloat16)
    back = lax.dot_general(
        slopes,
        lax.all_gather(head[0], "dp", axis=0, tiled=True),
        (((1,), (1,)), ((), ())),
        preferred_element_type=jnp.float32,
    )
    weighted = back * gains_wide[None, :]
    grad_rows = (
        inverse * weighted
        - widened * inverse**3 * jnp.mean(weighted * widened, axis=1, keepdims=True)
    ).astype(jnp.bfloat16)
    grad_hidden = lax.all_to_all(
        grad_rows[:, None, :], "fsdp", split_axis=0, concat_axis=1, tiled=True
    )
    columns = piece_normed
    grad_head = lax.psum_scatter(
        lax.dot_general(
            columns, slopes, (((0,), (0,)), ((), ())), preferred_element_type=jnp.float32
        ).astype(jnp.bfloat16),
        "dp",
        scatter_dimension=0,
        tiled=True,
    ).astype(jnp.float32)
    return (loss, grad_hidden, grad_head[None])


def solution(mesh):
    placed = (
        P(("dp", "fsdp"), None, None),
        P("fsdp", "dp", None),
        P("fsdp", "dp"),
        P("dp", "fsdp"),
        P(),
    )
    return jax.shard_map(
        per_device,
        mesh=mesh,
        in_specs=placed,
        out_specs=(P(), P(("dp", "fsdp"), None, None), P("fsdp", "dp", None)),
        check_vma=False,
    )
```

profile of v0, /device:TPU:16, one launch (start us, length us, event | category | flops | bytes accessed | tf_op | source)
XLA Modules:
  0.0 361.5 jit_solution(9783056093855041760)
XLA Ops:
  7.2 4.1 %copy.16 = bf16[64,16,1024]{2,0,1:T(8,128)(2,1)} copy(bf16[64,16,1024]{2,1,0:T(8,128)(2,1)} %param.5) | data formatting | bytes 4194304 | tf_op args[0]
  11.3 9.2 %all-to-all-start = ((bf16[64,16,1024]{2,0,1:T(8,128)(2,1)}), bf16[64,16,1024]{2,0,1:T(8,128)(2,1)S(1)}, u32[]{:S(2)}, u32[]{:S(2)}) async-start(bf16[64,16,1024]{2,0,1:T(8,128)(2,1)} %copy.16), calls=%async_computation | async-start | bytes 4194304 | tf_op jit(solution)/shard_map/all_to_all | solution.py:10
  21.3 1.3 dynamic-slice
  23.5 79.2 %all-reduce = bf16[1024]{0:T(1024)(128)(2,1)S(1)} all-reduce(bf16[1024]{0:T(1024)(128)(2,1)S(1)} %dynamic-update-slice), channel_id=2, replica_groups=mesh['dp'=32,'fsdp'=16] {'dp'}, use_global_device_ids=true, to_apply=%add | all-reduce | flops 1024 | bytes 4096
  104.0 2.4 convert_element_type.61
  106.4 5.4 %copy.17 = f32[1024,1024]{0,1:T(8,128)} copy(f32[1024,1024]{1,0:T(8,128)} %bitcast.29) | data formatting | bytes 8388608 | tf_op jit(solution)/shard_map/convert_element_type | solution.py:19
  112.4 5.5 %fusion.9 = (f32[1024]{0:T(1024)S(1)}, f32[1024,1024]{0,1:T(8,128)S(1)}) fusion(bf16[1,1024,1024]{2,1,0:T(8,128)(2,1)} %all-gather.4.cloned.1.call-done, f32[1024,1024]{0,1:T(8,128)} %copy.17, f32[1024]{0:T(1024)S(1)} %convert_element_type.63, f32[1024]{0:T(1024)S(1)} %rsqrt.15), kind=kOutput, calls=%fused_computation.25 | convolution fusion | flops 2151676928 | bytes 10498048 | tf_op jit(solution)/shard_map/dot_general | solution.py:27
  117.9 1.1 fusion
  119.0 1.0 copy-done.1
  120.0 1.6 copy-done
  121.6 3.9 %convolution_convert_fusion = bf16[1024,1024]{1,0:T(8,128)(2,1)} fusion(f32[1024,1024]{0,1:T(8,128)S(1)} %copy-done, f32[1024]{0:T(1024)S(1)} %convert_element_type.63, f32[1024]{0:T(1024)S(1)} %rsqrt.15, f32[1024,1024]{0,1:T(8,128)S(1)} %get-tuple-element.14, f32[1024]{0:T(1024)S(1)} %get-tuple-element.9, f32[1024]{0:T(1024)S(1)} %fusion.6, ...), kind=kOutput, calls=%fused_computation.14 | convolution fusion | flops 2159017984 | bytes 10510336 | tf_op jit(solution)/shard_map/dot_general | solution.py:55
  125.5 8.6 %multiply_reduce_fusion = (f32[1024]{0:T(1024)S(1)}, f32[1024,1024]{0,1:T(8,128)}) fusion(f32[1024,1024]{0,1:T(8,128)} %copy.17, f32[1024]{0:T(1024)S(1)} %convert_element_type.63, f32[1024,1024]{0,1:T(8,128)} %copy-done.1, f32[1024]{0:T(1024)S(1)} %get-tuple-element.9, f32[1024]{0:T(1024)S(1)} %fusion.6, s32[1024]{0:T(1024)S(1)} %bitcast.33, ...), kind=kOutput, calls=%fused_computation.1 | convolution fusion | flops 2157968384 | bytes 14704640 | tf_op jit(solution)/shard_map/dot_general | solution.py:39
  134.1 4.3 %fusion.1 = bf16[1024,1,1024]{0,2,1:T(8,128)(2,1)S(1)} fusion(f32[1024,1024]{0,1:T(8,128)} %copy.17, f32[1024,1024]{0,1:T(8,128)} %get-tuple-element.16, f32[1024]{0:T(1024)S(1)} %convert_element_type.63, f32[1024]{0:T(1024)S(1)} %broadcast_multiply_fusion, f32[1024]{0:T(1024)S(1)} %multiply_multiply_fusion, f32[1024]{0:T(1024)S(1)} %rsqrt.15), kind=kLoop, calls=%fused_computation.9 | loop fusion | flops 6291456 | bytes 10502144 | tf_op jit(solution)/shard_map/broadcast_in_dim | solution.py:51
  138.9 2.8 reduce.3
  141.7 2.9 copy.23
  144.5 2.8 reshape.67
  147.3 7.3 %all-to-all-start.1 = ((bf16[16,2,32768]{2,1,0:T(2,128)(2,1)}), bf16[16,2,32768]{2,1,0:T(2,128)(2,1)S(1)}, u32[]{:S(2)}, u32[]{:S(2)}) async-start(bf16[16,2,32768]{2,1,0:T(2,128)(2,1)} %reshape.67), calls=%async_computation.1 | async-start | bytes 4194304 | tf_op jit(solution)/shard_map/all_to_all | solution.py:50
  155.2 1.3 select_reduce_fusion.1
  156.5 135.5 %psum.7 = f32[]{:T(128)} all-reduce(f32[]{:T(128)} %select_reduce_fusion.1), channel_id=1, replica_groups=mesh['dp'=32,'fsdp'=16] {'dp','fsdp'}, use_global_device_ids=true, to_apply=%region_6.7 | all-reduce | flops 1 | bytes 8 | tf_op jit(solution)/shard_map/psum | solution.py:35
  292.7 6.8 %reshape.68 = bf16[1024,1,1024]{2,1,0:T(2,128)(2,1)} reshape(bf16[16,2,32768]{2,1,0:T(2,128)(2,1)S(1)} %all-to-all-done.1) | data formatting | bytes 4194304
  299.4 3.0 copy.22
  302.5 2.5 copy.21
  304.9 47.1 %reduce-scatter.2.cloned.1.call-done = bf16[32,1024]{1,0:T(8,128)(2,1)} async-done(((bf16[1024,1024]{1,0:T(8,128)(2,1)}), bf16[32,1024]{1,0:T(8,128)(2,1)}) %reduce-scatter.2.cloned.1.call-update) | async-done | bytes 65552 | tf_op jit(solution)/shard_map/reduce_scatter | solution.py:54
  352.1 1.5 bitcast_convert_fusion
  (26 shorter events, 3.4 us)
Async XLA Ops:
  7.2 16.1 %copy-start.4 = (bf16[1,32]{1,0:T(2,128)(2,1)S(1)}, bf16[1,32]{1,0:T(2,128)(2,1)}, u32[]{:S(2)}) copy-start(bf16[1,32]{1,0:T(2,128)(2,1)} %param.7) | copy-start | bytes 196
  7.2 95.5 %copy-start.3 = (s32[32]{0:T(128)S(1)}, s32[32]{0:T(128)}, u32[]{:S(2)}) copy-start(s32[32]{0:T(128)} %param.9) | copy-start | bytes 388
  11.3 92.7 %all-to-all-start = ((bf16[64,16,1024]{2,0,1:T(8,128)(2,1)}), bf16[64,16,1024]{2,0,1:T(8,128)(2,1)S(1)}, u32[]{:S(2)}, u32[]{:S(2)}) async-start(bf16[64,16,1024]{2,0,1:T(8,128)(2,1)} %copy.16), calls=%async_computation | async-start | bytes 4194304 | tf_op jit(solution)/shard_map/all_to_all | solution.py:10
  20.5 91.9 %all-gather.4.cloned.1.call-start = ((), (), s32[]{:S(2)}) async-start(), calls=%async_computation.4 | async-start | bytes 2162688 | tf_op jit(solution)/shard_map/all_gather | solution.py:22
  21.2 330.8 %reduce-scatter.2.cloned.1.call-start = ((), (), s32[]{:S(2)}) async-start(), calls=%async_computation.3 | async-start | bytes 2162688 | tf_op jit(solution)/shard_map/reduce_scatter | solution.py:54
  112.4 5.5 %copy-start.2 = (s32[1024,1]{0,1:T(1,128)S(1)}, s32[1024,1]{0,1:T(1,128)}, u32[]{:S(2)}) copy-start(s32[1024,1]{0,1:T(1,128)} %param.8) | copy-start | bytes 12292
  117.9 2.1 copy-start.1
  117.9 3.7 %copy-start = (f32[1024,1024]{0,1:T(8,128)S(1)}, f32[1024,1024]{0,1:T(8,128)}, u32[]{:S(2)}) copy-start(f32[1024,1024]{0,1:T(8,128)} %copy.17) | copy-start | bytes 12582916
  147.3 145.4 %all-to-all-start.1 = ((bf16[16,2,32768]{2,1,0:T(2,128)(2,1)}), bf16[16,2,32768]{2,1,0:T(2,128)(2,1)S(1)}, u32[]{:S(2)}, u32[]{:S(2)}) async-start(bf16[16,2,32768]{2,1,0:T(2,128)(2,1)} %reshape.67), calls=%async_computation.1 | async-start | bytes 4194304 | tf_op jit(solution)/shard_map/all_to_all | solution.py:50
Sparse Core Ops, SparseCore 0:
  24.5 86.4 all-gather.3
  134.2 217.7 reduce-scatter.1
where the time goes:
time: 362 us
  blocking collectives  215 us (59%)
  waiting for transfers between devices  47.8 us (13%)
  local copies, waits for them, and re-layouts  32 us (9%)
  matrix products  18 us (5%)
  between operations  17.3 us (5%)
  starting transfers between devices  16.6 us (5%)
  other arithmetic  15.2 us (4%)
    psum x1, blocking collectives, per_device(): summed = lax.psum(local, ('dp', 'fsdp'))  136 us
    unnamed x1, blocking collectives  79.2 us
    reduce_scatter x1, waiting for transfers between devices, per_device(): lax.psum_scatter(lax.dot_general(columns, slopes, (((0,), (0,)), ((), ())...  47.1 us
    unnamed x19, local copies, waits for them, and re-layouts  26 us
    all_to_all x1, starting transfers between devices, per_device(): lax.all_to_all(hidden, 'fsdp', split_axis=1, concat_axis=0, tiled=True)  9.24 us
    dot_general x1, matrix products, per_device(): lax.dot_general(slopes, lax.all_gather(head[0], 'dp', axis=0, tiled=True)...  8.6 us
    all_to_all x1, starting transfers between devices, per_device(): lax.all_to_all(grad_rows[:, None, :], 'fsdp', split_axis=0, concat_axis=1...  7.27 us
  transfers between devices with their start and end apart: 4, of which 1 were waited for; matrix products, arithmetic and copies ran while one was open for 10% of the time, Pallas kernels for 0%

commit v1 on v0

v1 whole, which is shorter than its diff:
```python
import jax
import jax.numpy as jnp
from jax import lax
from jax.experimental import pallas as pl
from jax.experimental.pallas import tpu as pltpu
from jax.sharding import PartitionSpec as P

EPS = 1e-05
MESH = pl.DeviceIdType.MESH
NX, NZ, NY, NC = 4, 8, 8, 2
NF = NY * NC
E = 1024
CARD = 1024
CHUNK = 64
ROWS = E // (NX * NZ)
HALF = ROWS // 2
GA, GB = slice(0, 640), slice(640, CARD)
CA = 640
CB = CARD - CA
A, B = slice(0, CA), slice(CA, CARD)

RING_Y = (4, 3, 5, 2, 6, 1, 7)
RING_Z = (4, 3, 5, 2, 6, 1, 7)
RING_X = (2, 1, 3)
RIGHT, LEFT = 0, 1


def mm(a, b, ca, cb):
    return lax.dot_general(
        a, b, (((ca,), (cb,)), ((), ())), preferred_element_type=jnp.float32
    )


def column(row):
    n = row.shape[1]
    r = lax.broadcasted_iota(jnp.int32, (n, n), 0)
    c = lax.broadcasted_iota(jnp.int32, (n, n), 1)
    return jnp.sum(jnp.where(r == c, row, jnp.zeros_like(row)), axis=1, keepdims=True)


def kernel(
    hidden_ref, head_ref, gain_ref, labels_ref, lengths_ref,
    loss_ref, gout_ref, ghead_ref,
    hin, hd, gn, lab, lens, xs, xr, w, nb, sb, gs, dw, xrecv, xsum, zrecv,
    ring, bsum, brecv, sums, xb, xo, lacc, lf, lx, lz,
    hsem, isem, ex_s, ex_r, as_s, as_r,
    waz_s, waz_r, wax_s, wax_r, wbx_s, wbx_r, wbz_s, wbz_r,
    gs_s, gs_r, lsem, rax_s, rax_r, raz_s, raz_r, rbz_s, rbz_r, rbx_s, rbx_r,
    fin_s, fin_r, lfs_s, lfs_r, lxs_s, lxs_r, lzs_s, lzs_r,
):
    dp = lax.axis_index("dp")
    fs = lax.axis_index("fsdp")
    x, z = dp // NZ, lax.rem(dp, NZ)
    y, c = fs // NC, lax.rem(fs, NC)
    h = y // 4
    jme = lax.rem(y, 4) * NC + c

    def ring_y(off):
        return lax.rem(y + off, NY)

    def ring_x(off):
        return lax.rem(x + off, NX)

    def ring_z(off):
        return lax.rem(z + off, NZ)

    def dev_f(yy, cc):
        return (dp, yy * NC + cc)

    def dev_x(off):
        return (ring_x(off) * NZ + z, fs)

    def dev_z(zz):
        return (x * NZ + zz, fs)

    def remote(src, dst, send, recv, device):
        return pltpu.make_async_remote_copy(
            src, dst, send, recv, device_id=device, device_id_type=MESH
        )

    offs_f = [(o, d) for o in RING_Y for d in range(NC)] + [(0, 1)]

    def load(b):
        at = pl.ds(pl.multiple_of(b * 16, 16), 16)
        return pltpu.make_async_copy(hidden_ref.at[at], hin.at[at], hsem.at[b])

    small = [
        pltpu.make_async_copy(head_ref.at[0], hd, isem.at[0]),
        pltpu.make_async_copy(gain_ref, gn, isem.at[1]),
        pltpu.make_async_copy(labels_ref, lab.at[0], isem.at[2]),
        pltpu.make_async_copy(lengths_ref, lens, isem.at[3]),
    ]
    for b in range(4):
        load(b).start()
    for s in small:
        s.start()

    barrier = pltpu.get_barrier_semaphore()
    for o, d in offs_f:
        pl.semaphore_signal(
            barrier, inc=1, device_id=dev_f(ring_y(o), lax.rem(c + d, NC)), device_id_type=MESH
        )
    for o in RING_X:
        pl.semaphore_signal(barrier, inc=1, device_id=dev_x(o), device_id_type=MESH)
    for o in RING_Z:
        pl.semaphore_signal(barrier, inc=1, device_id=dev_z(ring_z(o)), device_id_type=MESH)

    for s in small:
        s.wait()

    gain = column(gn[...].astype(jnp.float32))
    w[0, x, z] = (hd[...].astype(jnp.float32) * gain).astype(jnp.bfloat16)

    r = lax.broadcasted_iota(jnp.int32, (256, 256), 0)
    q = lax.broadcasted_iota(jnp.int32, (256, 256), 1)
    perm = (q == (r & 15) * 16 + (r >> 4)).astype(jnp.bfloat16)

    def split(b, carry):
        at = pl.ds(pl.multiple_of(b * 16, 16), 16)
        load(b).wait()
        block = hin[at].reshape(256, E)
        xs[:, :, at, :] = mm(perm, block, 1, 0).astype(jnp.bfloat16).reshape(2, 8, 16, E)
        return carry

    lax.fori_loop(0, 4, split, 0)

    pl.semaphore_wait(barrier, len(offs_f) + len(RING_X) + len(RING_Z))

    anti = dev_f(ring_y(4), c)
    ex = [
        remote(w.at[0, x, z], w.at[1, x, z], ex_s.at[0], ex_r.at[0], anti),
        remote(lab.at[0], lab.at[1], ex_s.at[1], ex_r.at[1], anti),
    ]
    for e in ex:
        e.start()

    far = 2 + 4 * c
    targets = (
        [(0, 1 - c, c)]
        + [(1, d, 2 + c) for d in range(NC)]
        + [(7, d, 4 + c) for d in range(NC)]
        + [(far, d, 6 + c) for d in range(NC)]
    )

    def a2a(i):
        off, cc, slot = targets[i]
        yy = ring_y(off)
        return remote(
            xs.at[:, lax.rem(yy, 4) * NC + cc], xr.at[:, slot],
            as_s.at[i], as_r.at[slot], dev_f(yy, cc),
        )

    def a2a_in(slot):
        return remote(xr.at[:, slot], xr.at[:, slot], as_s.at[0], as_r.at[slot], dev_f(y, 1 - c))

    def z_way(way):
        return dev_z(ring_z(1 if way == RIGHT else 7))

    def az(role, k, way):
        zz = ring_z(NZ - k) if way == RIGHT else ring_z(k)
        ref = w.at[role, x, zz, :, GA]
        if k == 3:
            ref = w.at[role, x, zz, pl.ds(HALF * way, HALF), GA]
        i = 2 * k + way
        return remote(ref, ref, waz_s.at[role, i], waz_r.at[role, i], z_way(way))

    def ax(role, off, i):
        ref = w.at[role, x, ring_z(off), :, GA]
        n = 3 * off + i
        return remote(ref, ref, wax_s.at[role, n], wax_r.at[role, n], dev_x(RING_X[i]))

    def bx(role, i):
        ref = w.at[role, x, z, :, GB]
        return remote(ref, ref, wbx_s.at[role, i], wbx_r.at[role, i], dev_x(RING_X[i]))

    def bz(role, k, way):
        zz = ring_z(NZ - k) if way == RIGHT else ring_z(k)
        ref = w.at[role, :, zz, :, GB]
        if k == 3:
            ref = w.at[role, pl.ds(2 * way, 2), zz, :, GB]
        i = 2 * k + way
        return remote(ref, ref, wbz_s.at[role, i], wbz_r.at[role, i], z_way(way))

    WAYS = (RIGHT, LEFT)

    def gather(role):
        for way in WAYS:
            az(role, 0, way).start()
        for i in range(3):
            bx(role, i).start()
        for i in range(3):
            ax(role, 0, i).start()

    def az_step(role, k):
        for way in WAYS:
            az(role, k - 1, way).wait_recv()
            if k < 4:
                az(role, k, way).start()
                for i in range(3):
                    ax(role, NZ - k if way == RIGHT else k, i).start()
        if k == 4:
            for i in range(3):
                ax(role, 4, i).start()

    def bz_step(role, k):
        if k == 0:
            for i in range(3):
                bx(role, i).wait_recv()
        for way in WAYS:
            if k > 0:
                bz(role, k - 1, way).wait_recv()
            bz(role, k, way).start()

    def gathered(role):
        for off in range(NZ):
            for i in range(3):
                ax(role, off, i).wait_recv()
        for way in WAYS:
            bz(role, 3, way).wait_recv()

    gather(0)
    for i in (5, 6, 1, 2, 3, 4, 0):
        a2a(i).start()
    xr[:, c] = xs[:, jme]
    az_step(0, 1)
    bz_step(0, 0)
    az_step(0, 2)
    bz_step(0, 1)
    az_step(0, 3)
    ex[0].wait_recv()
    gather(1)
    az_step(0, 4)
    bz_step(0, 2)
    az_step(1, 1)
    bz_step(1, 0)
    az_step(1, 2)
    bz_step(0, 3)
    az_step(1, 3)
    bz_step(1, 1)
    az_step(1, 4)
    ex[1].wait_recv()
    bz_step(1, 2)
    bz_step(1, 3)

    length = lens[dp]
    lacc[...] = jnp.zeros_like(lacc)
    chips = [ring_y(o) for o in (0, 7, 1, 6, 2)]
    lanes = lax.broadcasted_iota(jnp.int32, (1, 128), 1)

    def by_slot(of):
        rows = [of(yy) for yy in chips]
        rows = rows[:3] + [jnp.where(lanes < CHUNK, rows[3], rows[4])]
        return jnp.concatenate([column(row) for row in rows], axis=0)

    frames = by_slot(lambda yy: yy * 128 + lanes)
    valid = (frames < length).astype(jnp.float32)

    sources = [(0, 1 - c, 1 - c)] + [
        (o, d, s) for o, d, s in
        ((7, 0, 2), (7, 1, 3), (1, 0, 4), (1, 1, 5), (6, 0, 6), (2, 1, 7))
    ]

    def half(p):
        return h if p == 0 else 1 - h

    def out(p, i):
        off, cc, slot = sources[i]
        return remote(
            gs.at[p, slot], gout_ref.at[half(p), jme], gs_s.at[p, i], gs_r.at[half(p), jme],
            dev_f(ring_y(off), cc),
        )

    def out_in(p, i):
        j = lax.rem(jme + i, 8)
        return remote(gs.at[p, 0], gout_ref.at[p, j], gs_s.at[p, 0], gs_r.at[p, j], dev_f(y, 1 - c))

    def out_own(p):
        return pltpu.make_async_copy(gs.at[p, c], gout_ref.at[half(p), jme], lsem.at[p])

    def position(p):
        rows = xr[half(p)].reshape(512, E).astype(jnp.float32)
        inverse = lax.rsqrt(jnp.mean(rows * rows, axis=1, keepdims=True) + EPS)
        scaled = rows * inverse
        scaled_b = scaled.astype(jnp.bfloat16)
        nb[...] = scaled_b
        weights = w[p].reshape(E, CARD)
        logits = mm(scaled_b, weights, 1, 0)
        top = jnp.max(logits, axis=1, keepdims=True)
        powers = jnp.exp(logits - top)
        total = jnp.sum(powers, axis=1, keepdims=True)
        labels = by_slot(lambda yy: lab[p, pl.ds(yy, 1), :])
        hit = lax.broadcasted_iota(jnp.int32, (512, CARD), 1) == labels
        picked = jnp.sum(jnp.where(hit, logits, 0.0), axis=1, keepdims=True)
        token = valid * (top + jnp.log(total) - picked)
        lacc[...] += jnp.broadcast_to(jnp.sum(token, axis=0, keepdims=True), (8, 128))
        probs = powers * (valid / total)
        slopes = jnp.where(hit, probs - valid, probs).astype(jnp.bfloat16)
        sb[...] = slopes
        back = mm(slopes, weights, 1, 1)
        mean = jnp.mean(back * scaled, axis=1, keepdims=True)
        gs[p] = (inverse * (back - scaled * mean)).astype(jnp.bfloat16).reshape(8, CHUNK, E)
        for i in (5, 6, 1, 2, 3, 4, 0):
            out(p, i).start()
        out_own(p).start()

    def products(p):
        for xt in range(NX):
            part = mm(nb[:, 256 * xt : 256 * (xt + 1)], sb[...], 0, 0)
            dw[p, xt] = part.astype(jnp.bfloat16).reshape(NZ, ROWS, CARD)

    zg = z // 2

    def group(g):
        return lax.rem(zg + g, 4)

    def rax(role, g, i):
        n = 3 * g + i
        return remote(
            dw.at[role, ring_x(RING_X[i]), pl.ds(2 * group(g), 2), :, A],
            xrecv.at[role, i, pl.ds(2 * g, 2)],
            rax_s.at[role, n], rax_r.at[role, n], dev_x(RING_X[i]),
        )

    def raz(role, g, k):
        return remote(
            xsum.at[role, 2 * g + k], zrecv.at[role, z],
            raz_s.at[role, 2 * g + k], raz_r.at[role, z], dev_z(2 * group(g) + k),
        )

    def raz_own(role):
        k = 1 - lax.rem(z, 2)
        return remote(
            xsum.at[role, k], zrecv.at[role, z], raz_s.at[role, k], raz_r.at[role, z],
            dev_z(2 * zg + k),
        )

    def raz_in(role, i):
        zz = ring_z(i)
        return remote(
            xsum.at[role, 0], zrecv.at[role, zz], raz_s.at[role, 0], raz_r.at[role, zz],
            dev_z(zz),
        )

    def add_x(role, g):
        for i in range(3):
            rax(role, g, i).wait_recv()
        part = dw[role, x, pl.ds(2 * group(g), 2), :, A].astype(jnp.float32)
        for i in range(3):
            part = part + xrecv[role, i, 2 * g : 2 * g + 2].astype(jnp.float32)
        xsum[role, 2 * g : 2 * g + 2] = part.astype(jnp.bfloat16)
        if g:
            for k in range(2):
                raz(role, g, k).start()
        else:
            raz_own(role).start()

    def total_a(role):
        for i in range(1, NZ):
            raz_in(role, i).wait_recv()
        acc = xsum[role, lax.rem(z, 2)].astype(jnp.float32)
        for i in range(1, NZ):
            acc = acc + zrecv[role, ring_z(i)].astype(jnp.float32)
        return acc

    def rbz(role, k, way):
        t = ring_z(4 - k + NZ) if way == RIGHT else ring_z(4 + k)
        half_x = pl.ds(2 * way, 2)
        i = 2 * k + way
        if k == 0:
            src, dst = dw.at[role, half_x, t, :, B], ring.at[role, way, 0, half_x]
        else:
            src, dst = ring.at[role, way, k - 1], ring.at[role, way, k]
        return remote(src, dst, rbz_s.at[role, i], rbz_r.at[role, i], z_way(way))

    def ring_step(role, k):
        for way in WAYS:
            t = ring_z(4 - k + NZ) if way == RIGHT else ring_z(4 + k)
            rbz(role, k - 1, way).wait_recv()
            at = pl.ds(2 * way, 2) if k == 1 else pl.ds(0, 4)
            part = ring[role, way, k - 1, at].astype(jnp.float32)
            part = part + dw[role, at, t, :, B].astype(jnp.float32)
            ring[role, way, k - 1, at] = part.astype(jnp.bfloat16)
            if k == 1:
                at = pl.ds(2 - 2 * way, 2)
                ring[role, way, 0, at] = dw[role, at, t, :, B]
            rbz(role, k, way).start()

    def rbx(role, i):
        return remote(
            bsum.at[role, ring_x(RING_X[i])], brecv.at[role, i],
            rbx_s.at[role, i], rbx_r.at[role, i], dev_x(RING_X[i]),
        )

    def ring_last(role):
        block = dw[role, :, z, :, B].astype(jnp.float32)
        for way in WAYS:
            rbz(role, 3, way).wait_recv()
            block = block + ring[role, way, 3].astype(jnp.float32)
        bsum[role] = block.astype(jnp.bfloat16)
        for i in range(3):
            rbx(role, i).start()

    def total_b(role):
        acc = bsum[role, x].astype(jnp.float32)
        for i in range(3):
            rbx(role, i).wait_recv()
            acc = acc + brecv[role, i].astype(jnp.float32)
        return acc

    def scatter(role):
        for way in WAYS:
            rbz(role, 0, way).start()
        for g in (2, 1, 3, 0):
            for i in range(3):
                rax(role, g, i).start()

    a2a_in(1 - c).wait_recv()
    for slot in range(2, 8):
        a2a_in(slot).wait_recv()
    gathered(1)
    position(1)
    products(1)
    scatter(1)
    gathered(0)
    position(0)
    ring_step(1, 1)
    products(0)
    scatter(0)

    def loss_f(off, d):
        i = off * NC + d
        return remote(
            lf.at[fs], lf.at[fs], lfs_s.at[i], lfs_r.at[i],
            dev_f(ring_y(off), lax.rem(c + d, NC)),
        )

    def loss_x(i):
        return remote(lx.at[x], lx.at[x], lxs_s.at[i], lxs_r.at[i], dev_x(RING_X[i]))

    def loss_z(i):
        return remote(lz.at[z], lz.at[z], lzs_s.at[i], lzs_r.at[i], dev_z(ring_z(RING_Z[i])))

    lf[fs] = lacc[...]
    for o, d in offs_f:
        loss_f(o, d).start()
    add_x(1, 2)
    ring_step(1, 2)
    ring_step(0, 1)
    add_x(1, 1)
    ring_step(1, 3)
    ring_step(0, 2)
    add_x(1, 3)
    for o, d in offs_f:
        loss_f(o, d).wait()
    total_f = lf[0]
    for i in range(1, NF):
        total_f = total_f + lf[i]
    lx[x] = total_f
    for i in range(3):
        loss_x(i).start()
    ring_last(1)
    ring_step(0, 3)
    add_x(1, 0)
    xb[:, B] = total_b(1).astype(jnp.bfloat16)
    add_x(0, 2)
    for i in range(3):
        loss_x(i).wait()
    total_x = lx[0]
    for i in range(1, NX):
        total_x = total_x + lx[i]
    lz[z] = total_x
    for i in range(7):
        loss_z(i).start()
    xb[:, A] = total_a(1).astype(jnp.bfloat16)
    fin = remote(xb, xo, fin_s, fin_r, anti)
    fin.start()
    for e in ex:
        e.wait_send()
    for i in range(7):
        a2a(i).wait_send()
    for role in range(2):
        for k in range(4):
            for way in WAYS:
                az(role, k, way).wait_send()
                bz(role, k, way).wait_send()
        for i in range(3):
            bx(role, i).wait_send()
            for off in range(NZ):
                ax(role, off, i).wait_send()

    add_x(0, 1)
    ring_last(0)
    add_x(0, 3)
    add_x(0, 0)
    sums[:, B] = total_b(0)
    sums[:, A] = total_a(0)
    for i in range(7):
        loss_z(i).wait()
    total_z = lz[0]
    for i in range(1, NZ):
        total_z = total_z + lz[i]
    tokens = lens[0]
    for i in range(1, NX * NZ):
        tokens = tokens + lens[i]
    count = jnp.full((8, 128), tokens, jnp.int32).astype(jnp.float32) * NF
    loss_ref[...] = (total_z / count)[0:1, 0:1]

    fin.wait()
    ghead_ref[0] = (sums[...] + xo[...].astype(jnp.float32)) * gain

    for role in range(2):
        for k in range(4):
            for way in WAYS:
                rbz(role, k, way).wait_send()
        for i in range(3):
            rbx(role, i).wait_send()
            for g in range(4):
                rax(role, g, i).wait_send()
        for g in range(1, 4):
            for k in range(2):
                raz(role, g, k).wait_send()
        raz_own(role).wait_send()
    for p in range(2):
        for i in range(7):
            out(p, i).wait_send()
        for i in range(1, 8):
            out_in(p, i).wait_recv()
        out_own(p).wait()


def per_device(hidden, head, gain, targets, lengths):
    labels = targets.reshape(NY, 128)
    vmem = pl.BlockSpec(memory_space=pltpu.VMEM)
    hbm = pl.BlockSpec(memory_space=pltpu.HBM)
    bf = lambda *s: pltpu.VMEM(s, jnp.bfloat16)
    f32 = lambda *s: pltpu.VMEM(s, jnp.float32)
    dma = lambda *s: pltpu.SemaphoreType.DMA(s)
    one = pltpu.SemaphoreType.DMA
    pair = lambda *s: [dma(*s), dma(*s)]
    loss, grad, grad_head = pl.pallas_call(
        kernel,
        out_shape=(
            jax.ShapeDtypeStruct((1, 1), jnp.float32),
            jax.ShapeDtypeStruct((2, 8, CHUNK, E), jnp.bfloat16),
            jax.ShapeDtypeStruct((1, ROWS, CARD), jnp.float32),
        ),
        in_specs=[hbm] * 5,
        out_specs=(vmem, pl.BlockSpec(memory_space=pl.ANY), vmem),
        scratch_shapes=[
            bf(CHUNK, NF, E), bf(ROWS, CARD), bf(1, ROWS),
            pltpu.VMEM((2, NY, 128), jnp.int32), pltpu.SMEM((NX * NZ,), jnp.int32),
            bf(2, 8, CHUNK, E), bf(2, 8, CHUNK, E), bf(2, NX, NZ, ROWS, CARD),
            bf(512, E), bf(512, CARD), bf(2, 8, CHUNK, E), bf(2, NX, NZ, ROWS, CARD),
            bf(2, 3, NZ, ROWS, CA), bf(2, NZ, ROWS, CA), bf(2, NZ, ROWS, CA),
            bf(2, 2, 4, NX, ROWS, CB), bf(2, NX, ROWS, CB), bf(2, 3, ROWS, CB),
            f32(ROWS, CARD), bf(ROWS, CARD), bf(ROWS, CARD),
            f32(8, 128), f32(NF, 8, 128), f32(NX, 8, 128), f32(NZ, 8, 128),
            dma(4), dma(4), *pair(2), dma(7), dma(8),
            *pair(2, 8), *pair(2, 24), *pair(2, 3), *pair(2, 8),
            dma(2, 7), dma(2, 8), dma(2), *pair(2, 12), *pair(2, 8), *pair(2, 8), *pair(2, 3),
            one, one, *pair(16), *pair(3), *pair(7),
        ],
        compiler_params=pltpu.CompilerParams(
            collective_id=0, has_side_effects=True, vmem_limit_bytes=46 << 20
        ),
        cost_estimate=pl.CostEstimate(
            flops=6 * 1024**3, bytes_accessed=4 << 20, transcendentals=1 << 20
        ),
    )(*(pltpu.with_memory_space_constraint(a, pltpu.HBM) for a in (hidden, head, gain, labels, lengths)))
    grad = jnp.transpose(grad.reshape(NF, CHUNK, E), (1, 0, 2))
    return loss[0, 0], grad, grad_head


def solution(mesh):
    placed = (
        P(("dp", "fsdp"), None, None),
        P("fsdp", "dp", None),
        P("fsdp", "dp"),
        P("dp", "fsdp"),
        P(),
    )
    return jax.shard_map(
        per_device,
        mesh=mesh,
        in_specs=placed,
        out_specs=(P(), P(("dp", "fsdp"), None, None), P("fsdp", "dp", None)),
        check_vma=False,
    )
```

time: 362 us -> 101 us (0.28)
  the two profiles are of different devices: /device:TPU:16 before, /device:TPU:64 now
where the time goes in v1:
time: 101 us; the launch traced here: 100 us
  Pallas kernels  94.9 us (94%)
  local copies, waits for them, and re-layouts  3.13 us (3%)
  between operations  2.33 us (2%)
    pallas_call x1, Pallas kernels, per_device(): pl.pallas_call(kernel, out_shape=(jax.ShapeDtypeStruct((1, 1), jnp.float3...  94.9 us
    reshape x1, local copies, waits for them, and re-layouts, per_device(): grad = jnp.transpose(grad.reshape(NF, CHUNK, E), (1, 0, 2))  2.47 us

profile of v1, /device:TPU:64, one launch (start us, length us, event | category | flops | bytes accessed | tf_op | source)
XLA Modules:
  0.0 100.4 jit_solution(291577126052722788)
XLA Ops:
  0.6 94.9 %shard_map.76 = (f32[1,1]{1,0:T(1,128)}, bf16[2,8,64,1024]{3,2,1,0:T(8,128)(2,1)S(1)}, f32[1,32,1024]{2,1,0:T(8,128)S(1)}) custom-call(bf16[64,16,1024]{2,1,0:T(8,128)(2,1)} %hidden_ref.1, bf16[1,32,1024]{2,1,0:T(8,128)(2,1)} %head_ref.1, bf16[1,32]{1,0:T(2,128)(2,1)} %gain_ref.1, s32[8,128]{1,0:T(8,128)} %bitcast.8, s32[32]{0:T(128)} %lengths_ref.1), custom_call_target="tpu_custom_call" | custom-call | flops 6442450944 | bytes 4194304 | tf_op jit(solution)/shard_map/pallas_call | solution.py:540
  95.6 2.5 %copy.10 = bf16[16,64,1024]{2,0,1:T(8,128)(2,1)} copy(bf16[16,64,1024]{2,1,0:T(8,128)(2,1)S(1)} %bitcast.6) | data formatting | bytes 4194304 | tf_op jit(solution)/shard_map/reshape | solution.py:570
  98.6 0.7 copy.14
